TPU v7x, 256 devices: a whole 4x4x8 slice. The times are simulated.
256 devices in a mesh: row: 16 (over x, y_hi, core), col: 16 (over z, y_lo).
Axes of the slice: x: 4, y: 4 (y_hi: 2, y_lo: 2; y = y_hi * 2 + y_lo), z: 8, core: 2. Of those that a mesh axis runs over, the one named last changes fastest.
Arguments:
- activations: bfloat16 [1024, 8192], P(None, 'row'), may hold values from -10 to 10
- cotangents: bfloat16 [1024, 8192], P(None, 'row'), may hold values from -10 to 10
- act_factor: bfloat16 [8192, 8192], P('row', 'col'), may hold values from -0.5 to 1.5
- grad_factor: bfloat16 [8192, 8192], P('row', 'col'), may hold values from -0.5 to 1.5
Outputs:
- act_updated: bfloat16 [8192, 8192], P('row', 'col')
- grad_updated: bfloat16 [8192, 8192], P('row', 'col')
All inputs are finite; a program needn't handle non-finite values.
Results may differ from a plain program's by a relative error of at most 0.0057.
Values may be sent and summed in bfloat16 or wider, within the bound.
No kernel may reach another device: no remote copies, remote signals or barrier semaphores. Data moves between devices by JAX's collectives and lax.ppermute only.
A program may use at most 64 MiB of HBM per device.

v0:
```python
import jax
import jax.numpy as jnp
from jax import lax
from jax.sharding import PartitionSpec as P

D = 8192
TOKENS = 1024
keep_scale = 1.45
gram_scale = 0.5


def times_transposed(factor_block, projected):
    return lax.dot_general(
        factor_block, projected, (((1,), (1,)), ((), ())), preferred_element_type=jnp.float32
    )


def local(activations, cotangents, act_factor, grad_factor):
    width = act_factor.shape[1]
    own_rows = lax.psum_scatter(
        jnp.concatenate(
            [
                jnp.dot(activations, act_factor, preferred_element_type=jnp.float32),
                jnp.dot(cotangents, grad_factor, preferred_element_type=jnp.float32),
            ],
            axis=1,
        ),
        "row",
        scatter_dimension=0,
        tiled=True,
    ).astype(jnp.bfloat16)
    projected = lax.all_gather(own_rows, "row", axis=0, tiled=True)
    squares = jnp.square(own_rows.astype(jnp.float32))
    act_total, grad_total = lax.psum(
        (jnp.sum(squares[:, :width]), jnp.sum(squares[:, width:])), ("row", "col")
    )
    act_mean = act_total / (TOKENS * D)
    grad_mean = grad_total / (TOKENS * D)
    act_proj = projected[:, :width]
    grad_proj = projected[:, width:]
    act_image, grad_image = lax.psum(
        (times_transposed(act_factor, act_proj), times_transposed(grad_factor, grad_proj)), "col"
    )
    act_image = act_image.astype(jnp.bfloat16)
    grad_image = grad_image.astype(jnp.bfloat16)
    act_change = jnp.dot(act_image, act_proj, preferred_element_type=jnp.float32)
    grad_change = jnp.dot(grad_image, grad_proj, preferred_element_type=jnp.float32)
    act_updated = (
        keep_scale * act_factor.astype(jnp.float32) - gram_scale * grad_mean / TOKENS * act_change
    ).astype(jnp.bfloat16)
    grad_updated = (
        keep_scale * grad_factor.astype(jnp.float32) - gram_scale * act_mean / TOKENS * grad_change
    ).astype(jnp.bfloat16)
    return (act_updated, grad_updated)


def solution(mesh):
    return jax.shard_map(
        local,
        mesh=mesh,
        in_specs=(P(None, "row"), P(None, "row"), P("row", "col"), P("row", "col")),
        out_specs=(P("row", "col"), P("row", "col")),
        check_vma=False,
    )
```

profile of v0, /device:TPU:16, one launch (start us, length us, event | category | flops | bytes accessed | tf_op | source)
XLA Modules:
  0.0 387.5 jit_solution(4529226681538673235)
XLA Ops:
  7.2 0.0 copy-start
  7.2 0.0 copy-start.3
  7.2 0.0 copy-start.5
  7.2 0.0 reduce-scatter.4.cloned.1.call-start
  7.2 1.1 copy-done
  8.4 1.8 fusion.10
  10.2 0.8 fusion.11
  11.0 2.5 pad_maximum_fusion
  13.5 5.3 %copy.7 = f32[1024,1024]{1,0:T(8,128)} copy(f32[1024,1024]{0,1:T(8,128)} %pad_maximum_fusion) | data formatting | bytes 8388608
  18.8 0.0 reduce-scatter.4.cloned.1.call-update
  18.8 0.0 all-gather.2.cloned.1.call-start
  18.9 89.7 %reduce-scatter.4.cloned.1.call-done = f32[64,1024]{1,0:T(8,128)} async-done(((f32[1024,1024]{1,0:T(8,128)}), f32[64,1024]{1,0:T(8,128)}) %reduce-scatter.4.cloned.1.call-update) | async-done | bytes 262160
  108.6 1.1 copy.8
  109.7 0.8 copy.6
  110.5 0.0 all-gather.2.cloned.1.call-update
  110.6 0.7 slice_reduce_fusion
  111.3 75.7 %all-reduce = (f32[]{:T(128)}, f32[]{:T(128)}) all-reduce(f32[]{:T(128)} %get-tuple-element.3, f32[]{:T(128)} %get-tuple-element.2), channel_id=1, replica_groups=mesh['row'=16,'col'=16] {'row','col'}, use_global_device_ids=true, to_apply=%region_2.0 | all-reduce | flops 2 | bytes 16 | tf_op jit(solution)/shard_map/psum | solution.py:34
  188.2 0.0 all-gather.2.cloned.1.call-done
  188.2 2.2 convolution_bitcast_fusion
  190.5 0.0 copy-done.1
  190.5 3.1 convolution_bitcast_fusion.1
  193.6 182.2 %all-reduce.3 = (bf16[512,1024]{0,1:T(8,128)(2,1)}, bf16[512,1024]{0,1:T(8,128)(2,1)}) all-reduce(f32[512,1024]{0,1:T(8,128)} %convolution_bitcast_fusion.1, f32[512,1024]{0,1:T(8,128)S(1)} %convolution_bitcast_fusion), channel_id=1, replica_groups=mesh['row'=16,'col'=16] {'col'}, use_global_device_ids=true, to_apply=%region_3.0 | all-reduce | flops 1048576 | bytes 6291456 | tf_op jit(solution)/shard_map/psum | solution.py:41
  375.8 3.4 fusion.2
  379.1 1.5 fusion.3
  (10 shorter events, 0.1 us)
Async XLA Ops:
  7.2 1.2 copy-start
  7.2 3.0 copy-start.3
  7.2 3.0 copy-start.5
  7.2 101.4 %reduce-scatter.4.cloned.1.call-start = ((), (), s32[]{:S(2)}) async-start(), calls=%async_computation.2 | async-start | bytes 4456448
  18.8 169.4 %all-gather.2.cloned.1.call-start = ((), (), s32[]{:S(2)}) async-start(), calls=%async_computation.1 | async-start | bytes 2228224 | tf_op jit(solution)/shard_map/all_gather | solution.py:32
  188.2 2.3 copy-start.1
  375.8 3.4 copy-start.2
  375.8 3.4 copy-start.4
  375.8 3.4 copy-start.6
Sparse Core Ops, SparseCore 0:
  19.0 89.6 reduce-scatter.3
  112.2 51.1 all-gather.1
where the time goes:
time: 388 us
  blocking collectives  258 us (66%)
  waiting for transfers between devices  89.8 us (23%)
  between operations  15.3 us (4%)
  matrix products  12.8 us (3%)
  local copies, waits for them, and re-layouts  8.43 us (2%)
    psum x1, blocking collectives, local(): lax.psum((times_transposed(act_factor, act_proj), times_transposed(grad_f...  182 us
    unnamed x3, waiting for transfers between devices  89.8 us
    psum x1, blocking collectives, local(): lax.psum((jnp.sum(squares[:, :width]), jnp.sum(squares[:, width:])), ('ro...  75.7 us
  transfers between devices with their start and end apart: 2, of which 1 were waited for; matrix products, arithmetic and copies ran while one was open for 0% of the time, Pallas kernels for 0%

commit v1 on v0

--- a/solution.py
+++ b/solution.py
@@ -2,6 +2,7 @@
 import jax.numpy as jnp
 from jax import lax
 from jax.sharding import PartitionSpec as P
+from jax.lax import psum
 
 D = 8192
 TOKENS = 1024
@@ -31,8 +32,8 @@
     ).astype(jnp.bfloat16)
     projected = lax.all_gather(own_rows, "row", axis=0, tiled=True)
     squares = jnp.square(own_rows.astype(jnp.float32))
-    act_total, grad_total = lax.psum(
-        (jnp.sum(squares[:, :width]), jnp.sum(squares[:, width:])), ("row", "col")
+    act_total, grad_total = psum(
+        psum((jnp.sum(squares[:, :width]), jnp.sum(squares[:, width:])), "row"), "col"
     )
     act_mean = act_total / (TOKENS * D)
     grad_mean = grad_total / (TOKENS * D)

time: 388 us -> 369 us (0.951)
  blocking collectives: 258 us -> 213 us
  waiting for transfers between devices: 89.8 us -> 112 us
    psum x1, blocking collectives: 75.7 us -> 30 us  [local(): psum((jnp.sum(squares[:, :width]), jnp.sum(squares[:, width:])), 'row')]
    all_gather x1, waiting for transfers between devices: 0.02 us -> 22.1 us  [local(): projected = lax.all_gather(own_rows, 'row', axis=0, tiled=True)]
  transfers between devices with their start and end apart: 2 -> 2, of which waited for: 1 -> 2; matrix products, arithmetic and copies ran while one was open for 0% -> 0% of each run, Pallas kernels for 0% -> 0%
where the time goes in v1:
time: 369 us; the launch traced here: 365 us
  blocking collectives  213 us (58%)
  waiting for transfers between devices  112 us (30%)
  between operations  15.4 us (4%)
  matrix products  12.8 us (3%)
  local copies, waits for them, and re-layouts  8.44 us (2%)
    psum x1, blocking collectives, local(): lax.psum((times_transposed(act_factor, act_proj), times_transposed(grad_f...  183 us
    unnamed x3, waiting for transfers between devices  89.8 us
    psum x1, blocking collectives, local(): psum((jnp.sum(squares[:, :width]), jnp.sum(squares[:, width:])), 'row')  30 us
    all_gather x1, waiting for transfers between devices, local(): projected = lax.all_gather(own_rows, 'row', axis=0, tiled=True)  22.1 us
    unnamed x16, local copies, waits for them, and re-layouts  7.65 us
  transfers between devices with their start and end apart: 2, of which 2 were waited for; matrix products, arithmetic and copies ran while one was open for 0% of the time, Pallas kernels for 0%

profile of v1, /device:TPU:16, one launch (start us, length us, event | category | flops | bytes accessed | tf_op | source)
XLA Modules:
  0.0 365.1 jit_solution(6173727388618705415)
XLA Ops:
  7.2 0.0 copy-start
  7.2 0.0 copy-start.3
  7.2 0.0 copy-start.5
  7.2 0.0 reduce-scatter.4.cloned.1.call-start
  7.2 1.1 copy-done
  8.4 1.8 fusion.10
  10.2 0.8 fusion.11
  11.0 2.5 pad_maximum_fusion
  13.5 5.3 %copy.7 = f32[1024,1024]{1,0:T(8,128)} copy(f32[1024,1024]{0,1:T(8,128)} %pad_maximum_fusion) | data formatting | bytes 8388608
  18.8 0.0 reduce-scatter.4.cloned.1.call-update
  18.8 0.0 all-gather.2.cloned.1.call-start
  18.9 89.7 %reduce-scatter.4.cloned.1.call-done = f32[64,1024]{1,0:T(8,128)} async-done(((f32[1024,1024]{1,0:T(8,128)}), f32[64,1024]{1,0:T(8,128)}) %reduce-scatter.4.cloned.1.call-update) | async-done | bytes 262160
  108.6 1.1 copy.8
  109.7 0.8 copy.6
  110.5 0.0 all-gather.2.cloned.1.call-update
  110.6 0.7 slice_reduce_fusion
  111.3 30.0 %all-reduce.1 = (f32[]{:T(128)}, f32[]{:T(128)}) all-reduce(f32[]{:T(128)} %get-tuple-element.3, f32[]{:T(128)} %get-tuple-element.2), channel_id=1, replica_groups=mesh['row'=16,'col'=16] {'row'}, use_global_device_ids=true, to_apply=%region_2.0 | all-reduce | flops 2 | bytes 16 | tf_op jit(solution)/shard_map/psum | solution.py:36
  141.3 22.1 %all-gather.2.cloned.1.call-done = bf16[1024,1024]{1,0:T(8,128)(2,1)} async-done(((bf16[64,1024]{1,0:T(8,128)(2,1)}), bf16[1024,1024]{1,0:T(8,128)(2,1)}) %all-gather.2.cloned.1.call-update) | async-done | bytes 2097168 | tf_op jit(solution)/shard_map/all_gather | solution.py:33
  163.4 2.2 convolution_bitcast_fusion
  165.6 3.1 convolution_bitcast_fusion.1
  168.7 183.3 %all-reduce.3 = (bf16[512,1024]{0,1:T(8,128)(2,1)}, f32[]{:T(128)}, bf16[512,1024]{0,1:T(8,128)(2,1)}, f32[]{:T(128)}) all-reduce(f32[512,1024]{0,1:T(8,128)} %convolution_bitcast_fusion.1, f32[]{:T(128)} %get-tuple-element.8, f32[512,1024]{0,1:T(8,128)S(1)} %convolution_bitcast_fusion, ...), channel_id=1, replica_groups=mesh['row'=16,'col'=16] {'col'}, use_global_device_ids=true, to_apply=%region_4.0 | all-reduce | flops 1048578 | bytes 6291472 | tf_op jit(solution)/shard_map/psum | solution.py:42
  353.3 0.0 copy-start.4
  353.3 3.4 fusion.2
  356.7 1.5 fusion.3
  (10 shorter events, 0.1 us)
Async XLA Ops:
  7.2 1.2 copy-start
  7.2 3.0 copy-start.3
  7.2 3.0 copy-start.5
  7.2 101.4 %reduce-scatter.4.cloned.1.call-start = ((), (), s32[]{:S(2)}) async-start(), calls=%async_computation.2 | async-start | bytes 4456448
  18.8 144.6 %all-gather.2.cloned.1.call-start = ((), (), s32[]{:S(2)}) async-start(), calls=%async_computation.1 | async-start | bytes 2228224 | tf_op jit(solution)/shard_map/all_gather | solution.py:33
  163.4 2.2 copy-start.1
  353.3 3.4 copy-start.2
  353.3 3.4 copy-start.4
  353.3 3.4 copy-start.6
Sparse Core Ops, SparseCore 0:
  19.0 89.6 reduce-scatter.3
  112.2 51.0 all-gather.1
